TPU v7x, 32 devices: a whole 2x2x4 slice. The times are simulated.
32 devices in a mesh: tiles: 2 (over y), band: 4 (over x, core), head: 4 (over z).
Axes of the slice: x: 2, y: 2, z: 4, core: 2. Of those that a mesh axis runs over, the one named last changes fastest.
Arguments:
- tokens: bfloat16 [8192, 1024], P(('tiles', 'band')), parts along dimension 0, may hold values from -24 to 24
- w_query: bfloat16 [1024, 1024], P(None, 'head'), may hold values from -0.375 to 0.375
- w_key: bfloat16 [1024, 1024], P(None, 'head'), may hold values from -0.1875 to 0.1875
- w_value: bfloat16 [1024, 1024], P(None, 'head'), may hold values from -0.1875 to 0.1875
- w_out: bfloat16 [1024, 1024], P('head'), may hold values from -0.75 to 0.75
- block_mask: int32 [64, 32], P('tiles'), parts along dimension 0, may hold values from 0 to 1, as said below
Outputs:
- projected: bfloat16 [8192, 1024], P(('tiles', 'band', 'head')), parts along dimension 0
There are 2 independent parts, one for each index of `tiles`. A program takes and returns all parts, laid end to end along the dimension named above; an argument that names none is the same for every part. Nothing has to cross between parts.
Inputs may be any that keep to these rules, and one draw needn't show every extreme that they name: `block_mask`: entries are 0 or 1. Every query block may attend to at least one key block. Among the 8 key blocks of one band at most 6 are named by some query block, and some band has exactly 6.
All inputs are finite; a program needn't handle non-finite values.
Results may differ from a plain program's by a relative error of at most 0.02.
Values may be sent and summed in bfloat16 or wider, within the bound.
A program may use at most 128 MiB of HBM per device.

v0:
```python
import functools
import jax
import jax.numpy as jnp
from jax import lax
from jax.experimental import pallas as pl
from jax.experimental.pallas import tpu as pltpu
from jax.sharding import PartitionSpec as P

HD = 64
BLK = 128
KEEP = 6
UNROLL = 8
LOW = -1e30
SCALE = HD**-0.5 * 1.4426950408889634
MIB = 1 << 20
BF16 = jnp.bfloat16
F32 = jnp.float32
NT = (((1,), (1,)), ((), ()))
TN = (((0,), (0,)), ((), ()))


def greet(peers):
    barrier = pltpu.get_barrier_semaphore()
    for peer in peers:
        pl.semaphore_signal(barrier, inc=1, device_id=peer, device_id_type=pl.DeviceIdType.MESH)


def all_greeted(peers):
    pl.semaphore_wait(pltpu.get_barrier_semaphore(), len(peers))


def make_plan(mask, group, nb, nh, work, turns):
    n_rows, n_kb = mask.shape
    per_band = n_kb // nb
    nq = per_band * nh
    t_max = work.shape[1]
    i32 = jnp.int32
    everything = mask[...].astype(F32)
    rows = mask[pl.ds(group * nq, nq), :].astype(F32)
    named = jnp.max(everything, axis=0, keepdims=True)
    left = lax.broadcasted_iota(i32, (n_kb, n_kb), 0)
    right = lax.broadcasted_iota(i32, (n_kb, n_kb), 1)
    below = (left < right).astype(F32)
    same = (left // per_band == right // per_band).astype(F32)
    rank = jnp.dot(named, below * same, preferred_element_type=F32)
    band = (lax.broadcasted_iota(i32, (1, n_kb), 1) // per_band).astype(F32)
    key = band * KEEP + jnp.minimum(rank, KEEP - 1.0)
    pos = jnp.dot(rows, below, preferred_element_type=F32)
    count = jnp.sum(rows, axis=1, keepdims=True)
    chunks = jnp.floor((count + 1.0) * 0.5)
    qi = lax.broadcasted_iota(i32, (nq, nq), 0)
    qj = lax.broadcasted_iota(i32, (nq, nq), 1)
    begin = jnp.dot(
        (qj < qi).astype(F32), jnp.broadcast_to(chunks, (nq, 128)),
        preferred_element_type=F32, precision=lax.Precision.HIGHEST,
    )[:, :1]
    end = begin + chunks
    slot = jnp.where(rows > 0, begin * 2.0 + pos, -1.0).T
    keys = jnp.broadcast_to(key, (nq, n_kb)).T
    t = lax.broadcasted_iota(i32, (1, t_max), 1).astype(F32)
    first_key = jnp.zeros((n_kb, t_max), F32)
    second_key = jnp.zeros((n_kb, t_max), F32)
    has_second = jnp.zeros((n_kb, t_max), F32)
    for q in range(nq):
        at, value = slot[:, q : q + 1], keys[:, q : q + 1]
        even, odd = at == 2.0 * t, at == 2.0 * t + 1.0
        first_key = first_key + jnp.where(even, value, 0.0)
        second_key = second_key + jnp.where(odd, value, 0.0)
        has_second = has_second + jnp.where(odd, 1.0, 0.0)
    total = lambda x: jnp.sum(x, axis=0, keepdims=True)
    a, b, two = total(first_key), total(second_key), total(has_second)
    work[0:1, :] = total((end <= t).astype(F32)).astype(i32)
    work[1:2, :] = a.astype(i32)
    work[2:3, :] = jnp.where(two > 0, b, a).astype(i32)
    work[3:4, :] = total((begin == t).astype(F32)).astype(i32)
    work[4:5, :] = (1.0 - two).astype(i32)
    work[5:8, :] = jnp.zeros((3, t_max), i32)
    turns[...] = jnp.broadcast_to(
        jnp.floor((jnp.sum(chunks, axis=0, keepdims=True) + (UNROLL - 1.0)) * (1.0 / UNROLL)), (8, 128)
    ).astype(i32)


def select_blocks(mask, me, per_band):
    named = []
    for i in range(per_band):
        named.append(
            functools.reduce(jnp.maximum, [mask[r, me * per_band + i] for r in range(mask.shape[0])])
        )
    picks, rank = [0] * KEEP, 0
    for i in range(per_band):
        for k in range(min(i + 1, KEEP)):
            picks[k] = picks[k] + i * named[i] * (rank == k)
        rank = rank + named[i]
    return picks


def project_exchange(
    nb, nh, mask_s, mask_v, tok_hbm, wq_hbm, wk_hbm, wv_hbm,
    q_all, kv_all, work, turns,
    tok, wq, wk, wv, qs, kvs, send_kv, recv_kv, send_q, recv_q, own, load,
):
    loads = [
        pltpu.make_async_copy(a, b, load.at[i])
        for i, (a, b) in enumerate(((wk_hbm, wk), (wv_hbm, wv), (tok_hbm, tok), (wq_hbm, wq)))
    ]
    for c in loads:
        c.start()
    me = lax.axis_index("band")
    group, place = me // nh, lax.rem(me, nh)
    nq = tok.shape[0]
    others = [lax.rem(me + d, nb) for d in range(1, nb)]
    greet([{"band": p} for p in others])
    sel = select_blocks(mask_s, me, nq)
    for c in loads[:3]:
        c.wait()

    for k in range(KEEP):
        rows = tok[sel[k]]
        keys = jnp.dot(rows, wk[...], preferred_element_type=F32)
        vals = jnp.dot(rows, wv[...], preferred_element_type=F32)
        for h in range(nh):
            cut = slice(h * HD, (h + 1) * HD)
            kvs[h, k] = jnp.concatenate([keys[:, cut], vals[:, cut]], axis=1).astype(BF16)
    all_greeted(others)

    def kv_copy(peer, origin):
        return pltpu.make_async_remote_copy(
            src_ref=kvs.at[lax.rem(peer, nh)],
            dst_ref=kv_all.at[pl.ds(origin * KEEP, KEEP)],
            send_sem=send_kv.at[peer],
            recv_sem=recv_kv.at[origin],
            device_id={"band": peer},
            device_id_type=pl.DeviceIdType.MESH,
        )

    order = [p for _, p in sorted(zip([abs(d - nb // 2) for d in range(1, nb)], range(nb - 1)))]
    for i in order:
        kv_copy(others[i], me).start()
    own_kv = pltpu.make_async_copy(kvs.at[place], kv_all.at[pl.ds(me * KEEP, KEEP)], own.at[0])
    own_kv.start()

    loads[3].wait()
    for m in range(nq // 2):
        two = jnp.dot(
            jnp.concatenate([tok[2 * m], tok[2 * m + 1]], axis=0), wq[...], preferred_element_type=F32
        )
        for h in range(nh):
            cut = slice(h * HD, (h + 1) * HD)
            qs[h, m] = jnp.concatenate([two[:BLK, cut], two[BLK:, cut]], axis=1).astype(BF16)

    def q_copy(to, origin):
        return pltpu.make_async_remote_copy(
            src_ref=qs.at[to],
            dst_ref=q_all.at[origin],
            send_sem=send_q.at[to],
            recv_sem=recv_q.at[origin],
            device_id={"band": group * nh + to},
            device_id_type=pl.DeviceIdType.MESH,
        )

    mates = [lax.rem(place + d, nh) for d in range(1, nh)]
    order_q = [i for _, i in sorted(zip([abs(d - nh // 2) for d in range(1, nh)], range(nh - 1)))]
    for i in order_q:
        q_copy(mates[i], place).start()
    own_q = pltpu.make_async_copy(qs.at[place], q_all.at[place], own.at[1])
    own_q.start()
    make_plan(mask_v, group, nb, nh, work, turns)
    own_kv.wait()
    own_q.wait()
    for p in others:
        kv_copy(p, me).wait_send()
        kv_copy(p, p).wait_recv()
    for p in mates:
        q_copy(p, place).wait_send()
        q_copy(p, p).wait_recv()


def attend(work, turns, q_in, kv, out, q_pad, v_t):
    n_kv, n_pair = kv.shape[0], q_in.shape[0]

    def prepare_kv(c, _):
        v_t[c] = kv[c].T[HD:]
        return 0

    lax.fori_loop(0, n_kv, prepare_kv, 0, unroll=4)
    zeros = jnp.zeros((HD, BLK), BF16)

    def prepare_q(m, _):
        two = q_in[m].T
        q_pad[2 * m] = jnp.concatenate([two[:HD], zeros], axis=0)
        q_pad[2 * m + 1] = jnp.concatenate([two[HD:], zeros], axis=0)
        return 0

    lax.fori_loop(0, n_pair, prepare_q, 0, unroll=2)
    q_pad[2 * n_pair] = jnp.zeros((BLK, BLK), BF16)

    def turn(i, state):
        peak, mass, total = state
        parts = []
        for u in range(UNROLL):
            t = i * UNROLL + u
            q, pair = work[0, t], (work[1, t], work[2, t])
            scores = [jnp.dot(kv[c], q_pad[q], preferred_element_type=F32) * SCALE for c in pair]
            top = functools.reduce(jnp.maximum, [jnp.max(x, axis=0, keepdims=True) for x in scores])
            weights = [jnp.exp2(x - top) for x in scores]
            part = functools.reduce(jnp.add, [jnp.sum(x, axis=0, keepdims=True) for x in weights])
            got = functools.reduce(
                jnp.add,
                [jnp.dot(v_t[c], x.astype(BF16), preferred_element_type=F32) for c, x in zip(pair, weights)],
            )
            parts.append((q, work[3, t], work[4, t], top, part, got))
        for q, first, repeat, top, part, got in parts:
            before = jnp.where(first > 0, LOW, peak)
            peak = jnp.maximum(before, top)
            f = jnp.exp2(before - peak)
            g = jnp.exp2(top - peak) * jnp.where(repeat > 0, 0.5, 1.0)
            mass = mass * f + part * g
            total = total * f + got * g
            out[q] = (total * (1.0 / mass)).astype(BF16)
        return peak, mass, total

    start = (jnp.full((1, BLK), LOW, F32), jnp.zeros((1, BLK), F32), jnp.zeros((HD, BLK), F32))
    lax.fori_loop(0, turns[0, 0], turn, start)


def exchange_project(nh, nz, att, w_hbm, out, got, w_full, send, recv, own):
    band, z = lax.axis_index("band"), lax.axis_index("head")
    group, place = band // nh, lax.rem(band, nh)
    n = nh * nz
    me = z * nh + place
    per = got.shape[1]
    per_band = per * nz
    others = [lax.rem(me + d, n) for d in range(1, n)]
    where = lambda p: {"band": group * nh + lax.rem(p, nh), "head": p // nh}
    w_load = pltpu.make_async_copy(w_hbm, w_full, own.at[1])
    w_load.start()
    greet([where(p) for p in others])
    all_greeted(others)

    def piece(p):
        return att.at[pl.ds(lax.rem(p, nh) * per_band + (p // nh) * per, per)]

    def copy(peer, origin):
        return pltpu.make_async_remote_copy(
            src_ref=piece(peer),
            dst_ref=got.at[origin],
            send_sem=send.at[peer],
            recv_sem=recv.at[origin],
            device_id=where(peer),
            device_id_type=pl.DeviceIdType.MESH,
        )

    for _, i in sorted(zip([abs(d - n // 2) for d in range(1, n)], range(n - 1))):
        copy(others[i], me).start()
    mine = pltpu.make_async_copy(piece(me), got.at[me], own.at[0])
    mine.start()
    mine.wait()
    w_load.wait()
    for p in others:
        copy(p, me).wait_send()
        copy(p, p).wait_recv()
    for r in range(per):
        heads = jnp.concatenate([got[i, r] for i in range(n)], axis=0)
        out[pl.ds(r * BLK, BLK), :] = lax.dot_general(
            heads, w_full[...], TN, preferred_element_type=F32
        ).astype(BF16)


def on_device(nb, nz, tokens, w_query, w_key, w_value, w_out, block_mask):
    nh = w_query.shape[1] // HD
    tok_rows = tokens.shape[0]
    nq = tok_rows // BLK
    per = nq // nz
    vmem = pl.BlockSpec(memory_space=pltpu.VMEM)
    smem = pl.BlockSpec(memory_space=pltpu.SMEM)
    hbm = pl.BlockSpec(memory_space=pl.ANY)
    dma = pltpu.SemaphoreType.DMA
    w_full = lax.all_gather(w_out, "head", axis=0, tiled=True)
    t_max = nh * nq * ((nb * KEEP + 1) // 2)
    t_max = -(-t_max // 128) * 128
    q_all, kv_all, work, turns = pl.pallas_call(
        functools.partial(project_exchange, nb, nh),
        out_shape=(
            jax.ShapeDtypeStruct((nh, nq // 2, BLK, BLK), BF16),
            jax.ShapeDtypeStruct((nb * KEEP, BLK, BLK), BF16),
            jax.ShapeDtypeStruct((8, t_max), jnp.int32),
            jax.ShapeDtypeStruct((8, 128), jnp.int32),
        ),
        in_specs=[smem, vmem, hbm, hbm, hbm, hbm],
        out_specs=(hbm, hbm, vmem, vmem),
        scratch_shapes=[
            pltpu.VMEM((nq, BLK, tokens.shape[1]), BF16),
            pltpu.VMEM(w_query.shape, BF16),
            pltpu.VMEM(w_key.shape, BF16),
            pltpu.VMEM(w_value.shape, BF16),
            pltpu.VMEM((nh, nq // 2, BLK, BLK), BF16),
            pltpu.VMEM((nh, KEEP, BLK, BLK), BF16),
            dma((nb,)),
            dma((nb,)),
            dma((nh,)),
            dma((nh,)),
            dma((2,)),
            dma((4,)),
        ],
        compiler_params=pltpu.CompilerParams(
            collective_id=0, has_side_effects=True, vmem_limit_bytes=32 * MIB
        ),
        name="project_exchange",
    )(block_mask, block_mask, tokens.reshape(nq, BLK, -1), w_query, w_key, w_value)
    att = pl.pallas_call(
        attend,
        out_shape=jax.ShapeDtypeStruct((nh * nq + 1, HD, BLK), BF16),
        in_specs=[smem, smem, vmem, vmem],
        out_specs=vmem,
        scratch_shapes=[
            pltpu.VMEM((nh * nq + 1, BLK, BLK), BF16),
            pltpu.VMEM((nb * KEEP, HD, BLK), BF16),
        ],
        compiler_params=pltpu.CompilerParams(vmem_limit_bytes=32 * MIB),
        name="attend",
    )(work, turns, q_all.reshape(nh * nq // 2, BLK, BLK), kv_all)
    n = nh * nz
    return pl.pallas_call(
        functools.partial(exchange_project, nh, nz),
        out_shape=jax.ShapeDtypeStruct((per * BLK, w_out.shape[1]), BF16),
        in_specs=[hbm, hbm],
        out_specs=vmem,
        scratch_shapes=[
            pltpu.VMEM((n, per, HD, BLK), BF16),
            pltpu.VMEM((w_out.shape[0] * nz, w_out.shape[1]), BF16),
            dma((n,)),
            dma((n,)),
            dma((2,)),
        ],
        compiler_params=pltpu.CompilerParams(
            collective_id=1, has_side_effects=True, vmem_limit_bytes=32 * MIB
        ),
        name="exchange_project",
    )(att, w_full)


def solution(mesh):
    return jax.shard_map(
        functools.partial(on_device, mesh.shape["band"], mesh.shape["head"]),
        mesh=mesh,
        in_specs=(
            P(("tiles", "band"), None),
            P(None, "head"),
            P(None, "head"),
            P(None, "head"),
            P("head", None),
            P("tiles", None),
        ),
        out_specs=P(("tiles", "band", "head"), None),
        check_vma=False,
    )
```

profile of v0, /device:TPU:0, one launch (start us, length us, event | category | flops | bytes accessed | tf_op | source)
XLA Modules:
  0.0 82.4 jit_solution(6443806918551246883)
XLA Ops:
  6.5 0.0 all-gather.2.cloned.1.call-start
  6.5 0.7 all-gather.2.cloned.1.call-update
  7.3 0.0 copy-start
  7.3 1.6 %copy-done = bf16[1024,1024]{1,0:T(8,128)(2,1)S(1)} copy-done((bf16[1024,1024]{1,0:T(8,128)(2,1)S(1)}, bf16[1024,1024]{1,0:T(8,128)(2,1)}, u32[]{:S(2)}) %copy-start) | copy-done | bytes 2097176
  8.8 0.0 copy-start.2
  8.9 1.0 %copy-done.2 = bf16[1024,256]{1,0:T(8,128)(2,1)S(1)} copy-done((bf16[1024,256]{1,0:T(8,128)(2,1)S(1)}, bf16[1024,256]{1,0:T(8,128)(2,1)}, u32[]{:S(2)}) %copy-start.2) | copy-done | bytes 524312
  9.9 0.0 copy-start.3
  9.9 1.0 %copy-done.3 = bf16[1024,256]{1,0:T(8,128)(2,1)S(1)} copy-done((bf16[1024,256]{1,0:T(8,128)(2,1)S(1)}, bf16[1024,256]{1,0:T(8,128)(2,1)}, u32[]{:S(2)}) %copy-start.3) | copy-done | bytes 524312
  10.9 0.0 copy-start.4
  10.9 1.0 %copy-done.4 = bf16[1024,256]{1,0:T(8,128)(2,1)S(1)} copy-done((bf16[1024,256]{1,0:T(8,128)(2,1)S(1)}, bf16[1024,256]{1,0:T(8,128)(2,1)}, u32[]{:S(2)}) %copy-start.4) | copy-done | bytes 524312
  12.0 0.0 copy-start.5
  12.0 0.7 copy-done.5
  12.7 19.6 %project_exchange.1 = (bf16[4,4,128,128]{3,2,1,0:T(8,128)(2,1)S(1)}, bf16[24,128,128]{2,1,0:T(8,128)(2,1)S(1)}, s32[8,384]{1,0:T(8,128)S(1)}, s32[8,128]{1,0:T(8,128)S(1)}) custom-call(s32[32,32]{1,0:T(8,128)S(1)} %copy-done.5, s32[32,32]{1,0:T(8,128)S(1)} %copy-done.5, bf16[8,128,1024]{2,1,0:T(8,128)(2,1)S(1)} %bitcast.2, bf16[1024,256]{1,0:T(8,128)(2,1)S(1)} %copy-done.2, ...), custom_call_target="tpu_custom_call" | custom-call | tf_op jit(solution)/shard_map/project_exchange/pallas_call | solution.py:281
  32.3 11.4 %attend.1.att = bf16[33,64,128]{2,1,0:T(8,128)(2,1)S(1)} custom-call(s32[8,384]{1,0:T(8,128)S(1)} %get-tuple-element.9.work, s32[8,128]{1,0:T(8,128)S(1)} %get-tuple-element.10.turns, bf16[16,128,128]{2,1,0:T(8,128)(2,1)S(1)} %bitcast.3, bf16[24,128,128]{2,1,0:T(8,128)(2,1)S(1)} %get-tuple-element.12.kv), custom_call_target="tpu_custom_call" | custom-call | tf_op jit(solution)/shard_map/attend/pallas_call | solution.py:310
  43.7 13.9 %all-gather.2.cloned.1.call-done.w_hbm = bf16[1024,1024]{1,0:T(8,128)(2,1)} async-done(((bf16[256,1024]{1,0:T(8,128)(2,1)}), bf16[1024,1024]{1,0:T(8,128)(2,1)}) %all-gather.2.cloned.1.call-update) | async-done | bytes 2097168 | tf_op jit(solution)/shard_map/all_gather | solution.py:278
  57.6 0.0 copy-start.1
  57.6 1.6 %copy-done.1 = bf16[1024,1024]{1,0:T(8,128)(2,1)S(1)} copy-done((bf16[1024,1024]{1,0:T(8,128)(2,1)S(1)}, bf16[1024,1024]{1,0:T(8,128)(2,1)}, u32[]{:S(2)}) %copy-start.1) | copy-done | bytes 2097176
  59.2 15.6 %exchange_project.1 = bf16[256,1024]{1,0:T(8,128)(2,1)S(1)} custom-call(bf16[33,64,128]{2,1,0:T(8,128)(2,1)S(1)} %attend.1.att, bf16[1024,1024]{1,0:T(8,128)(2,1)S(1)} %copy-done.1), custom_call_target="tpu_custom_call" | custom-call | tf_op jit(solution)/shard_map/exchange_project/pallas_call | solution.py:323
  74.8 0.8 copy.8
Async XLA Ops:
  6.5 51.1 %all-gather.2.cloned.1.call-start = ((), (), s32[]{:S(2)}) async-start(), calls=%async_computation | async-start | bytes 2621440 | tf_op jit(solution)/shard_map/all_gather | solution.py:278
  7.3 1.6 %copy-start = (bf16[1024,1024]{1,0:T(8,128)(2,1)S(1)}, bf16[1024,1024]{1,0:T(8,128)(2,1)}, u32[]{:S(2)}) copy-start(bf16[1024,1024]{1,0:T(8,128)(2,1)} %param.6) | copy-start | bytes 6291460
  8.8 1.0 %copy-start.2 = (bf16[1024,256]{1,0:T(8,128)(2,1)S(1)}, bf16[1024,256]{1,0:T(8,128)(2,1)}, u32[]{:S(2)}) copy-start(bf16[1024,256]{1,0:T(8,128)(2,1)} %wq_hbm.1) | copy-start | bytes 1572868
  9.9 1.0 %copy-start.3 = (bf16[1024,256]{1,0:T(8,128)(2,1)S(1)}, bf16[1024,256]{1,0:T(8,128)(2,1)}, u32[]{:S(2)}) copy-start(bf16[1024,256]{1,0:T(8,128)(2,1)} %wk_hbm.1) | copy-start | bytes 1572868
  10.9 1.0 %copy-start.4 = (bf16[1024,256]{1,0:T(8,128)(2,1)S(1)}, bf16[1024,256]{1,0:T(8,128)(2,1)}, u32[]{:S(2)}) copy-start(bf16[1024,256]{1,0:T(8,128)(2,1)} %wv_hbm.1) | copy-start | bytes 1572868
  12.0 0.7 copy-start.5
  57.6 1.6 %copy-start.1 = (bf16[1024,1024]{1,0:T(8,128)(2,1)S(1)}, bf16[1024,1024]{1,0:T(8,128)(2,1)}, u32[]{:S(2)}) copy-start(bf16[1024,1024]{1,0:T(8,128)(2,1)} %all-gather.2.cloned.1.call-done.w_hbm) | copy-start | bytes 6291460
Sparse Core Ops, SparseCore 0:
  8.9 48.6 all-gather.1
where the time goes:
time: 82.8 us; the launch traced here: 82.4 us
  Pallas kernels  46.6 us (56%)
  waiting for transfers between devices  14.6 us (18%)
  between operations  13.4 us (16%)
  local copies, waits for them, and re-layouts  7.81 us (9%)
    pallas_call x1, Pallas kernels, on_device(): pl.pallas_call(functools.partial(project_exchange, nb, nh), out_shape=(ja...  19.6 us
    pallas_call x1, Pallas kernels, on_device(): pl.pallas_call(functools.partial(exchange_project, nh, nz), out_shape=jax...  15.6 us
    all_gather x1, waiting for transfers between devices, on_device(): w_full = lax.all_gather(w_out, 'head', axis=0, tiled=True)  13.9 us
    pallas_call x1, Pallas kernels, on_device(): pl.pallas_call(attend, out_shape=jax.ShapeDtypeStruct((nh * nq + 1, HD, B...  11.4 us
    unnamed x13, local copies, waits for them, and re-layouts  7.81 us
  transfers between devices with their start and end apart: 1, of which 1 were waited for; matrix products, arithmetic and copies ran while one was open for 0% of the time, Pallas kernels for 38%

commit v1 on v0

v1 whole, which is shorter than its diff:
```python
import functools
import jax
import jax.numpy as jnp
from jax import lax
from jax.experimental import pallas as pl
from jax.experimental.pallas import tpu as pltpu
from jax.sharding import PartitionSpec as P

HD = 64
BLK = 128
KEEP = 6
LOW = -float(2**100)
SCALE = HD**-0.5 * 1.4426950408889634
MIB = 1 << 20
BF16 = jnp.bfloat16
F32 = jnp.float32
I32 = jnp.int32
NT = (((1,), (1,)), ((), ()))
W = KEEP * BLK


def select_blocks(mask, me, per_band):
    named = []
    for i in range(per_band):
        named.append(
            functools.reduce(jnp.maximum, [mask[r, me * per_band + i] for r in range(mask.shape[0])])
        )
    picks, rank = [0] * KEEP, 0
    for i in range(per_band):
        for k in range(min(i + 1, KEEP)):
            picks[k] = picks[k] + i * named[i] * (rank == k)
        rank = rank + named[i]
    return picks


def make_bias(mask, me, nb, bias):
    n_rows, n_kb = mask.shape
    nq = n_kb // nb
    slots = bias.shape[1]
    everything = mask[...].astype(F32).T
    rows = mask[pl.ds(pl.multiple_of(me * nq, nq), nq), :].astype(F32)
    named = jnp.broadcast_to(jnp.max(everything, axis=1, keepdims=True), (n_kb, slots))
    left = lax.broadcasted_iota(I32, (n_kb, n_kb), 0)
    right = lax.broadcasted_iota(I32, (n_kb, n_kb), 1)
    earlier = ((right < left) & (left // nq == right // nq)).astype(F32)
    rank = jnp.dot(earlier, named, preferred_element_type=F32)
    band = (lax.broadcasted_iota(I32, (n_kb, slots), 0) // nq).astype(F32)
    slot = lax.broadcasted_iota(I32, (n_kb, slots), 1).astype(F32)
    place = jnp.where((slot == band * KEEP + rank) & (named > 0) & (rank < KEEP), 1.0, 0.0)
    allowed = jnp.dot(rows, place, preferred_element_type=F32)
    value = jnp.where(allowed > 0, 0.0, LOW)
    for i in range(nq):
        bias[i * BLK : (i + 1) * BLK, :] = jnp.broadcast_to(value[i : i + 1, :], (BLK, slots)).astype(BF16)


def layer(
    nt, nb, nz, mask_h, tok_h, wq_h, wk_h, wv_h, wo_h, out,
    mask_s, mask_v, tok, wq, wk, wv, rows_v, kv, q_pad, bias, onehot, top, acc, att, got, wo, pre,
    load, kv_send, kv_fwd, kv_recv, a_send, a_recv, w1_send, w2_send, w3_send, w_recv,
):
    nh = q_pad.shape[0]
    nq = tok.shape[0]
    n_chips = nb // 2
    slots = bias.shape[1]
    n_rows = nq * BLK
    depth = wo.shape[1]
    parts = 2 * nt
    per_part = depth // parts
    half = att.shape[2]
    tile, band, z = lax.axis_index("tiles"), lax.axis_index("band"), lax.axis_index("head")
    chip, core = band // 2, lax.rem(band, 2)
    sibling = chip * 2 + 1 - core
    mesh_id = pl.DeviceIdType.MESH

    pairs = ((mask_h, mask_s), (mask_h, mask_v), (tok_h, tok), (wk_h, wk), (wv_h, wv), (wq_h, wq), (wo_h, wo.at[z]))
    loads = [pltpu.make_async_copy(a, b, load.at[i]) for i, (a, b) in enumerate(pairs)]
    for c in loads:
        c.start()

    def chip_at(step):
        return lax.rem(chip + step, n_chips)

    peers = [{"band": sibling}]
    peers += [{"band": chip_at(d) * 2 + core} for d in range(1, n_chips)]
    peers += [{"head": lax.rem(z + d, nz)} for d in range(1, nz)]
    peers += [{"tiles": lax.rem(tile + d, nt)} for d in range(1, nt)]
    barrier = pltpu.get_barrier_semaphore()
    for p in peers:
        pl.semaphore_signal(barrier, inc=1, device_id=p, device_id_type=mesh_id)

    def remote(src, dst, send, recv, to):
        return pltpu.make_async_remote_copy(
            src_ref=src, dst_ref=dst, send_sem=send, recv_sem=recv, device_id=to, device_id_type=mesh_id
        )

    def kv_copy(h, origin, send, to):
        return remote(kv.at[h, origin], kv.at[h, origin], send, kv_recv.at[h, origin], {"band": to})

    def kv_direct(h, step):
        return kv_copy(h, band, kv_send.at[h, step], chip_at(step) * 2 + core)

    def kv_own(h):
        return kv_copy(h, band, kv_send.at[h, 0], sibling)

    def kv_forward(h, step):
        return kv_copy(h, chip_at(step) * 2 + core, kv_fwd.at[h, step], sibling)

    def kv_arrived(h, origin):
        kv_copy(h, origin, kv_recv.at[h, origin], sibling).wait_recv()

    def w_piece(source, part):
        return wo.at[source, pl.ds(pl.multiple_of(part * per_part, per_part), per_part)]

    my_part = tile * 2 + core

    def w_first(d):
        here = pl.ds(pl.multiple_of(my_part * per_part, per_part), per_part)
        return remote(
            wo_h.at[here], w_piece(z, my_part), w1_send.at[d], w_recv.at[z, my_part], {"head": lax.rem(z + d, nz)}
        )

    def w_second(d, t):
        source = lax.rem(z + d, nz)
        piece = w_piece(source, my_part)
        return remote(piece, piece, w2_send.at[d, t], w_recv.at[source, my_part], {"tiles": lax.rem(tile + t, nt)})

    def w_third(d, t):
        source, part = lax.rem(z + d, nz), lax.rem(tile + t, nt) * 2 + core
        piece = w_piece(source, part)
        return remote(piece, piece, w3_send.at[d, t], w_recv.at[source, part], {"band": sibling})

    def w_arrived(d, part):
        source = lax.rem(z + d, nz)
        piece = w_piece(source, part)
        remote(piece, piece, w1_send.at[d], w_recv.at[source, part], {"band": sibling}).wait_recv()

    slot_of = lax.broadcasted_iota(I32, (BLK, slots), 1)
    for s in range(nb * KEEP):
        onehot[s * BLK : (s + 1) * BLK, :] = jnp.where(slot_of == s, 1.0, 0.0).astype(BF16)
    loads[0].wait()
    sel = select_blocks(mask_s, band, nq)
    loads[1].wait()
    make_bias(mask_v, band, nb, bias)
    pl.semaphore_wait(barrier, len(peers))
    for d in range(1, nz):
        w_first(d).start()

    lane = lax.broadcasted_iota(I32, (1, BLK), 1)
    low_half = lane < HD

    loads[2].wait()
    for k in range(KEEP):
        rows_v[k * BLK : (k + 1) * BLK, :] = tok[sel[k]]
    loads[3].wait()
    loads[4].wait()
    for g in range(0, nh, 4):
        cols = slice(g * HD, min(g + 4, nh) * HD)
        keys = jnp.dot(rows_v[...], wk[:, cols], preferred_element_type=F32)
        vals = jnp.dot(rows_v[...], wv[:, cols], preferred_element_type=F32)
        for h in range(g, min(g + 4, nh)):
            cut = slice((h - g) * HD, (h - g + 1) * HD)
            kv[h, band] = jnp.concatenate([keys[:, cut], vals[:, cut]], axis=1).astype(BF16)
    for h in range(nh):
        if h < 2:
            for d in range(1, n_chips):
                kv_direct(h, d).start()
        kv_own(h).start()

    loads[5].wait()
    queries = jnp.dot(tok[...].reshape(n_rows, -1), wq[...], preferred_element_type=F32) * SCALE
    for h in range(nh):
        two = queries[:, (h // 2) * BLK : (h // 2 + 1) * BLK]
        if h % 2:
            two = pltpu.roll(two, HD, 1)
        q_pad[h] = jnp.where(low_half, two, 0.0).astype(BF16)

    tq = n_rows // 2

    def span(b):
        return pl.ds(pl.multiple_of(b * W, W), W)

    def score(h, b, i):
        r = slice(i * tq, (i + 1) * tq)
        q = jnp.concatenate([q_pad[h, r, :], bias[r, :]], axis=1)
        k = jnp.concatenate([kv[h, b], onehot[span(b), :]], axis=1)
        return lax.dot_general(q, k, NT, preferred_element_type=F32)

    def gather(s, h, b, i, first):
        r = slice(i * tq, (i + 1) * tq)
        cut = [s[:, j * BLK : (j + 1) * BLK] for j in range(KEEP)]
        m = jnp.broadcast_to(functools.reduce(jnp.maximum, cut).max(axis=1, keepdims=True), (tq, BLK))
        if not first:
            before = top[h, r, :]
            m = jnp.maximum(before, m)
        top[h, r, :] = m
        p = jnp.concatenate([jnp.exp2((x - m).astype(BF16)) for x in cut], axis=1)
        tile_kv = kv[h, b]
        v = jnp.where(low_half, jnp.ones_like(tile_kv), tile_kv)
        a = jnp.dot(p, v, preferred_element_type=F32)
        if not first:
            a = a + acc[h, r, :] * jnp.exp2(before - m)
        acc[h, r, :] = a

    def block(h, bands, first):
        units = [(b, i, first and n == 0) for n, b in enumerate(bands) for i in range(2)]
        s = score(h, *units[0][:2])
        for n, (b, i, start) in enumerate(units):
            after = score(h, *units[n + 1][:2]) if n + 1 < len(units) else None
            gather(s, h, b, i, start)
            s = after

    def local_block(h, _):
        @pl.when((h >= 1) & (h + 1 < nh))
        def _():
            for d in range(1, n_chips):
                kv_direct(h + 1, d).start()

        @pl.when(h == nh // 2)
        def _():
            for d in range(1, n_chips):
                kv_arrived(0, chip_at(d) * 2 + core)
                kv_forward(0, d).start()

        kv_arrived(h, sibling)
        block(h, (band, sibling), True)
        return 0

    lax.fori_loop(0, nh, local_block, 0)

    for d in range(1, nz):
        w_arrived(d, my_part)
        for t in range(nt):
            (w_second(d, t) if t else w_third(d, 0)).start()

    def a_copy(h, d):
        to = lax.rem(z + d, nz)
        return remote(att.at[h, to], got.at[h, z], a_send.at[h, d], a_recv.at[h, z], {"head": to})

    def a_arrived(h, d):
        origin = lax.rem(z + d, nz)
        remote(att.at[h, origin], got.at[h, origin], a_send.at[h, d], a_recv.at[h, origin], {"head": origin}).wait_recv()

    def far_block(h, _):
        @pl.when(h + 1 < nh)
        def _():
            for d in range(1, n_chips):
                kv_arrived(h + 1, chip_at(d) * 2 + core)
                kv_forward(h + 1, d).start()

        @pl.when(h == nh - 1)
        def _():
            for t in range(1, nt):
                for d in range(1, nz):
                    w_arrived(d, lax.rem(tile + t, nt) * 2 + core)
                    w_third(d, t).start()

        for d in range(1, n_chips):
            other = chip_at(d) * 2
            kv_arrived(h, other + 1 - core)
            block(h, (other + core, other + 1 - core), False)
        for p in range(nz):
            a0 = acc[h, p * 2 * half : p * 2 * half + half, :]
            a1 = acc[h, p * 2 * half + half : (p + 1) * 2 * half, :]
            value = jnp.where(low_half, pltpu.roll(a0, HD, 1), a1)
            mass = jnp.where(low_half, a0, pltpu.roll(a1, HD, 1))
            att[h, p] = (value / mass).astype(BF16)
        for d in range(1, nz):
            a_copy(h, d).start()
        got[h, z] = att[h, z]
        return 0

    lax.fori_loop(0, nh, far_block, 0)

    for t in range(nt):
        for d in range(1, nz):
            w_arrived(d, lax.rem(tile + t, nt) * 2 + 1 - core)
    loads[6].wait()

    def heads(hs):
        return jnp.concatenate(
            [
                jnp.concatenate([got[h, s][:, r * HD : (r + 1) * HD] for s in range(nz) for h in hs], axis=1)
                for r in range(2)
            ],
            axis=0,
        )

    def weights(hs):
        return jnp.concatenate([wo[s, hs[0] * HD : (hs[-1] + 1) * HD, :] for s in range(nz)], axis=0)

    early, last = list(range(nh - 1)), [nh - 1]
    for h in early:
        for d in range(1, nz):
            a_arrived(h, d)
    pre[...] = jnp.dot(heads(early), weights(early), preferred_element_type=F32)
    for d in range(1, nz):
        a_arrived(nh - 1, d)
    out[...] = (pre[...] + jnp.dot(heads(last), weights(last), preferred_element_type=F32)).astype(BF16)

    for h in range(nh):
        kv_own(h).wait_send()
        for d in range(1, n_chips):
            kv_direct(h, d).wait_send()
            kv_forward(h, d).wait_send()
        for d in range(1, nz):
            a_copy(h, d).wait_send()
    for d in range(1, nz):
        w_first(d).wait_send()
        for t in range(nt):
            w_third(d, t).wait_send()
            if t:
                w_second(d, t).wait_send()


def on_device(nt, nb, nz, tokens, w_query, w_key, w_value, w_out, block_mask):
    nh = w_query.shape[1] // HD
    n_rows, width = tokens.shape
    nq = n_rows // BLK
    out_rows = n_rows // nz
    slots = -(-nb * KEEP // 128) * 128
    hbm = pl.BlockSpec(memory_space=pl.ANY)
    vmem = pltpu.VMEM
    dma = pltpu.SemaphoreType.DMA
    return pl.pallas_call(
        functools.partial(layer, nt, nb, nz),
        out_shape=jax.ShapeDtypeStruct((out_rows, w_out.shape[1]), BF16),
        in_specs=[hbm] * 6,
        out_specs=pl.BlockSpec(memory_space=pltpu.VMEM),
        scratch_shapes=[
            pltpu.SMEM(block_mask.shape, I32),
            vmem(block_mask.shape, I32),
            vmem((nq, BLK, width), BF16),
            vmem(w_query.shape, BF16),
            vmem(w_key.shape, BF16),
            vmem(w_value.shape, BF16),
            vmem((W, width), BF16),
            vmem((nh, nb, W, 2 * HD), BF16),
            vmem((nh, n_rows, 2 * HD), BF16),
            vmem((n_rows, slots), BF16),
            vmem((nb * W, slots), BF16),
            vmem((nh, n_rows, 128), F32),
            vmem((nh, n_rows, 128), F32),
            vmem((nh, nz, out_rows // 2, 2 * HD), BF16),
            vmem((nh, nz, out_rows // 2, 2 * HD), BF16),
            vmem((nz,) + w_out.shape, BF16),
            vmem((out_rows, w_out.shape[1]), F32),
            dma((7,)),
            dma((nh, nb // 2)),
            dma((nh, nb // 2)),
            dma((nh, nb)),
            dma((nh, nz)),
            dma((nh, nz)),
            dma((nz,)),
            dma((nz, nt)),
            dma((nz, nt)),
            dma((nz, 2 * nt)),
        ],
        compiler_params=pltpu.CompilerParams(
            collective_id=0, has_side_effects=True, vmem_limit_bytes=58 * MIB
        ),
        name="layer",
    )(block_mask, tokens.reshape(nq, BLK, width), w_query, w_key, w_value, w_out)


def solution(mesh):
    return jax.shard_map(
        functools.partial(on_device, mesh.shape["tiles"], mesh.shape["band"], mesh.shape["head"]),
        mesh=mesh,
        in_specs=(
            P(("tiles", "band"), None),
            P(None, "head"),
            P(None, "head"),
            P(None, "head"),
            P("head", None),
            P("tiles", None),
        ),
        out_specs=P(("tiles", "band", "head"), None),
        check_vma=False,
    )
```

time: 82.8 us -> 38.2 us (0.46)
  waiting for transfers between devices: 14.6 us -> 0 us
  between operations: 13.4 us -> 0.01 us
  Pallas kernels: 46.6 us -> 36.1 us
  local copies, waits for them, and re-layouts: 7.81 us -> 1.87 us
    all_gather x1 -> x0, waiting for transfers between devices: 13.9 us -> none  [on_device(): w_full = lax.all_gather(w_out, 'head', axis=0, tiled=True)]
    pallas_call x3 -> x1, Pallas kernels: 46.6 us -> 36.1 us  [on_device(): pl.pallas_call(functools.partial(layer, nt, nb, nz), out_shape=jax.ShapeD...]
    unnamed x13 -> x1, local copies, waits for them, and re-layouts: 7.81 us -> 1.87 us
  transfers between devices with their start and end apart: 1 -> 0, of which waited for: 1 -> 0; matrix products, arithmetic and copies ran while one was open for 0% -> 0% of each run, Pallas kernels for 38% -> 0%
where the time goes in v1:
time: 38.2 us; the launch traced here: 38 us
  Pallas kernels  36.1 us (95%)
  local copies, waits for them, and re-layouts  1.87 us (5%)
    pallas_call x1, Pallas kernels, on_device(): pl.pallas_call(functools.partial(layer, nt, nb, nz), out_shape=jax.ShapeD...  36.1 us
    unnamed x1, local copies, waits for them, and re-layouts  1.87 us

profile of v1, /device:TPU:0, one launch (start us, length us, event | category | flops | bytes accessed | tf_op | source)
XLA Modules:
  0.0 38.0 jit_solution(3201963196556803627)
XLA Ops:
  0.0 36.1 %layer.1 = bf16[256,1024]{1,0:T(8,128)(2,1)} custom-call(s32[32,32]{1,0:T(8,128)} %mask_h.1, bf16[8,128,1024]{2,1,0:T(8,128)(2,1)} %bitcast.1, bf16[1024,256]{1,0:T(8,128)(2,1)} %wq_h.1, bf16[1024,256]{1,0:T(8,128)(2,1)} %wk_h.1, bf16[1024,256]{1,0:T(8,128)(2,1)} %wv_h.1, bf16[256,1024]{1,0:T(8,128)(2,1)} %wo_h.1), custom_call_target="tpu_custom_call" | custom-call | tf_op jit(solution)/shard_map/layer/pallas_call | solution.py:324
  36.1 1.9 %copy.8 = bf16[256,1024]{1,0:T(8,128)(2,1)} copy(bf16[256,1024]{1,0:T(8,128)(2,1)} %layer.1) | data formatting | bytes 1048576

commit v2 on v1

--- a/solution.py
+++ b/solution.py
@@ -55,7 +55,7 @@
 
 def layer(
     nt, nb, nz, mask_h, tok_h, wq_h, wk_h, wv_h, wo_h, out,
-    mask_s, mask_v, tok, wq, wk, wv, rows_v, kv, q_pad, bias, onehot, top, acc, att, got, wo, pre,
+    mask_s, mask_v, tok, wq, wk, wv, made, kv, q_pad, bias, onehot, top, acc, att, got, wo, pre,
     load, kv_send, kv_fwd, kv_recv, a_send, a_recv, w1_send, w2_send, w3_send, w_recv,
 ):
     nh = q_pad.shape[0]
@@ -139,8 +139,6 @@
         onehot[s * BLK : (s + 1) * BLK, :] = jnp.where(slot_of == s, 1.0, 0.0).astype(BF16)
     loads[0].wait()
     sel = select_blocks(mask_s, band, nq)
-    loads[1].wait()
-    make_bias(mask_v, band, nb, bias)
     pl.semaphore_wait(barrier, len(peers))
     for d in range(1, nz):
         w_first(d).start()
@@ -148,23 +146,25 @@
     lane = lax.broadcasted_iota(I32, (1, BLK), 1)
     low_half = lane < HD
 
-    loads[2].wait()
-    for k in range(KEEP):
-        rows_v[k * BLK : (k + 1) * BLK, :] = tok[sel[k]]
-    loads[3].wait()
-    loads[4].wait()
-    for g in range(0, nh, 4):
-        cols = slice(g * HD, min(g + 4, nh) * HD)
-        keys = jnp.dot(rows_v[...], wk[:, cols], preferred_element_type=F32)
-        vals = jnp.dot(rows_v[...], wv[:, cols], preferred_element_type=F32)
-        for h in range(g, min(g + 4, nh)):
-            cut = slice((h - g) * HD, (h - g + 1) * HD)
-            kv[h, band] = jnp.concatenate([keys[:, cut], vals[:, cut]], axis=1).astype(BF16)
-    for h in range(nh):
-        if h < 2:
-            for d in range(1, n_chips):
-                kv_direct(h, d).start()
-        kv_own(h).start()
+    for c in loads[2:5]:
+        c.wait()
+    for g in range(0, nh, 2):
+        cols = slice(g * HD, (g + 2) * HD)
+        both = jnp.dot(
+            tok[...].reshape(n_rows, -1), jnp.concatenate([wk[:, cols], wv[:, cols]], axis=1),
+            preferred_element_type=F32,
+        )
+        keys, vals = both[:, :BLK], both[:, BLK:]
+        made[0] = jnp.where(low_half, keys, pltpu.roll(vals, HD, 1)).astype(BF16).reshape(nq, BLK, BLK)
+        made[1] = jnp.where(low_half, pltpu.roll(keys, HD, 1), vals).astype(BF16).reshape(nq, BLK, BLK)
+        for h in range(2):
+            for k in range(KEEP):
+                kv[g + h, band, k * BLK : (k + 1) * BLK, :] = made[h, sel[k]]
+        for h in (g, g + 1):
+            if h < 2:
+                for d in range(1, n_chips):
+                    kv_direct(h, d).start()
+            kv_own(h).start()
 
     loads[5].wait()
     queries = jnp.dot(tok[...].reshape(n_rows, -1), wq[...], preferred_element_type=F32) * SCALE
@@ -174,6 +174,8 @@
             two = pltpu.roll(two, HD, 1)
         q_pad[h] = jnp.where(low_half, two, 0.0).astype(BF16)
 
+    loads[1].wait()
+    make_bias(mask_v, band, nb, bias)
     tq = n_rows // 2
 
     def span(b):
@@ -215,23 +217,12 @@
             for d in range(1, n_chips):
                 kv_direct(h + 1, d).start()
 
-        @pl.when(h == nh // 2)
-        def _():
-            for d in range(1, n_chips):
-                kv_arrived(0, chip_at(d) * 2 + core)
-                kv_forward(0, d).start()
-
         kv_arrived(h, sibling)
         block(h, (band, sibling), True)
         return 0
 
     lax.fori_loop(0, nh, local_block, 0)
 
-    for d in range(1, nz):
-        w_arrived(d, my_part)
-        for t in range(nt):
-            (w_second(d, t) if t else w_third(d, 0)).start()
-
     def a_copy(h, d):
         to = lax.rem(z + d, nz)
         return remote(att.at[h, to], got.at[h, z], a_send.at[h, d], a_recv.at[h, z], {"head": to})
@@ -241,23 +232,20 @@
         remote(att.at[h, origin], got.at[h, origin], a_send.at[h, d], a_recv.at[h, origin], {"head": origin}).wait_recv()
 
     def far_block(h, _):
-        @pl.when(h + 1 < nh)
+        @pl.when(h == 1)
         def _():
-            for d in range(1, n_chips):
-                kv_arrived(h + 1, chip_at(d) * 2 + core)
-                kv_forward(h + 1, d).start()
-
-        @pl.when(h == nh - 1)
-        def _():
-            for t in range(1, nt):
-                for d in range(1, nz):
-                    w_arrived(d, lax.rem(tile + t, nt) * 2 + core)
-                    w_third(d, t).start()
+            for d in range(1, nz):
+                w_arrived(d, my_part)
+                for t in range(nt):
+                    (w_second(d, t) if t else w_third(d, 0)).start()
 
         for d in range(1, n_chips):
-            other = chip_at(d) * 2
-            kv_arrived(h, other + 1 - core)
-            block(h, (other + core, other + 1 - core), False)
+            same = chip_at(d) * 2 + core
+            kv_arrived(h, same)
+            kv_forward(h, d).start()
+            block(h, (same,), False)
+            kv_arrived(h, chip_at(d) * 2 + 1 - core)
+            block(h, (chip_at(d) * 2 + 1 - core,), False)
         for p in range(nz):
             a0 = acc[h, p * 2 * half : p * 2 * half + half, :]
             a1 = acc[h, p * 2 * half + half : (p + 1) * 2 * half, :]
@@ -271,6 +259,10 @@
 
     lax.fori_loop(0, nh, far_block, 0)
 
+    for t in range(1, nt):
+        for d in range(1, nz):
+            w_arrived(d, lax.rem(tile + t, nt) * 2 + core)
+            w_third(d, t).start()
     for t in range(nt):
         for d in range(1, nz):
             w_arrived(d, lax.rem(tile + t, nt) * 2 + 1 - core)
@@ -318,7 +310,7 @@
     nq = n_rows // BLK
     out_rows = n_rows // nz
     slots = -(-nb * KEEP // 128) * 128
-    hbm = pl.BlockSpec(memory_space=pl.ANY)
+    hbm = pl.BlockSpec(memory_space=pltpu.HBM)
     vmem = pltpu.VMEM
     dma = pltpu.SemaphoreType.DMA
     return pl.pallas_call(
@@ -333,7 +325,7 @@
             vmem(w_query.shape, BF16),
             vmem(w_key.shape, BF16),
             vmem(w_value.shape, BF16),
-            vmem((W, width), BF16),
+            vmem((2, nq, BLK, 2 * HD), BF16),
             vmem((nh, nb, W, 2 * HD), BF16),
             vmem((nh, n_rows, 2 * HD), BF16),
             vmem((n_rows, slots), BF16),
@@ -356,7 +348,7 @@
             dma((nz, 2 * nt)),
         ],
         compiler_params=pltpu.CompilerParams(
-            collective_id=0, has_side_effects=True, vmem_limit_bytes=58 * MIB
+            collective_id=0, has_side_effects=True, vmem_limit_bytes=53 * MIB
         ),
         name="layer",
     )(block_mask, tokens.reshape(nq, BLK, width), w_query, w_key, w_value, w_out)

time: 38.2 us -> 35.6 us (0.932)
  Pallas kernels: 36.1 us -> 33.8 us
    pallas_call x1, Pallas kernels: 36.1 us -> 33.8 us  [on_device(): pl.pallas_call(functools.partial(layer, nt, nb, nz), out_shape=jax.ShapeD...]
    unnamed x1 -> x3, local copies, waits for them, and re-layouts: 1.87 us -> 1.51 us
where the time goes in v2:
time: 35.6 us; the launch traced here: 35.3 us
  Pallas kernels  33.8 us (95%)
  local copies, waits for them, and re-layouts  1.51 us (4%)
    pallas_call x1, Pallas kernels, on_device(): pl.pallas_call(functools.partial(layer, nt, nb, nz), out_shape=jax.ShapeD...  33.8 us
    unnamed x3, local copies, waits for them, and re-layouts  1.51 us

profile of v2, /device:TPU:0, one launch (start us, length us, event | category | flops | bytes accessed | tf_op | source)
XLA Modules:
  0.0 35.3 jit_solution(562410121593738815)
XLA Ops:
  0.0 0.0 copy-start
  0.0 0.7 %copy-done = s32[32,32]{1,0:T(8,128)S(1)} copy-done((s32[32,32]{1,0:T(8,128)S(1)}, s32[32,32]{1,0:T(8,128)}, u32[]{:S(2)}) %copy-start) | copy-done | bytes 4120
  0.7 33.8 %layer.1 = bf16[256,1024]{1,0:T(8,128)(2,1)S(1)} custom-call(s32[32,32]{1,0:T(8,128)S(1)} %copy-done, bf16[8,128,1024]{2,1,0:T(8,128)(2,1)} %bitcast.1, bf16[1024,256]{1,0:T(8,128)(2,1)} %wq_h.1, bf16[1024,256]{1,0:T(8,128)(2,1)} %wk_h.1, bf16[1024,256]{1,0:T(8,128)(2,1)} %wv_h.1, bf16[256,1024]{1,0:T(8,128)(2,1)} %wo_h.1), custom_call_target="tpu_custom_call" | custom-call | tf_op jit(solution)/shard_map/layer/pallas_call | solution.py:316
  34.5 0.8 %copy.8 = bf16[256,1024]{1,0:T(8,128)(2,1)} copy(bf16[256,1024]{1,0:T(8,128)(2,1)S(1)} %layer.1) | data formatting | bytes 1048576
Async XLA Ops:
  0.0 0.7 %copy-start = (s32[32,32]{1,0:T(8,128)S(1)}, s32[32,32]{1,0:T(8,128)}, u32[]{:S(2)}) copy-start(s32[32,32]{1,0:T(8,128)} %mask_h.1) | copy-start | bytes 12292

commit v3 on v2

--- a/solution.py
+++ b/solution.py
@@ -72,7 +72,9 @@
     sibling = chip * 2 + 1 - core
     mesh_id = pl.DeviceIdType.MESH
 
-    pairs = ((mask_h, mask_s), (mask_h, mask_v), (tok_h, tok), (wk_h, wk), (wv_h, wv), (wq_h, wq), (wo_h, wo.at[z]))
+    pairs = ((mask_h, mask_s), (mask_h, mask_v), (wk_h, wk), (wv_h, wv),
+             (tok_h.at[: nq // 2], tok.at[: nq // 2]), (tok_h.at[nq // 2 :], tok.at[nq // 2 :]),
+             (wq_h, wq), (wo_h, wo.at[z]))
     loads = [pltpu.make_async_copy(a, b, load.at[i]) for i, (a, b) in enumerate(pairs)]
     for c in loads:
         c.start()
@@ -146,17 +148,21 @@
     lane = lax.broadcasted_iota(I32, (1, BLK), 1)
     low_half = lane < HD
 
-    for c in loads[2:5]:
-        c.wait()
+    loads[2].wait()
+    loads[3].wait()
     for g in range(0, nh, 2):
         cols = slice(g * HD, (g + 2) * HD)
-        both = jnp.dot(
-            tok[...].reshape(n_rows, -1), jnp.concatenate([wk[:, cols], wv[:, cols]], axis=1),
-            preferred_element_type=F32,
-        )
-        keys, vals = both[:, :BLK], both[:, BLK:]
-        made[0] = jnp.where(low_half, keys, pltpu.roll(vals, HD, 1)).astype(BF16).reshape(nq, BLK, BLK)
-        made[1] = jnp.where(low_half, pltpu.roll(keys, HD, 1), vals).astype(BF16).reshape(nq, BLK, BLK)
+        weight = jnp.concatenate([wk[:, cols], wv[:, cols]], axis=1)
+        for i in range(2):
+            blocks = slice(i * nq // 2, (i + 1) * nq // 2)
+            if g == 0:
+                loads[4 + i].wait()
+            both = jnp.dot(tok[blocks].reshape(n_rows // 2, -1), weight, preferred_element_type=F32)
+            keys, vals = both[:, :BLK], both[:, BLK:]
+            one = jnp.where(low_half, keys, pltpu.roll(vals, HD, 1)).astype(BF16)
+            two = jnp.where(low_half, pltpu.roll(keys, HD, 1), vals).astype(BF16)
+            made[0, blocks] = one.reshape(nq // 2, BLK, BLK)
+            made[1, blocks] = two.reshape(nq // 2, BLK, BLK)
         for h in range(2):
             for k in range(KEEP):
                 kv[g + h, band, k * BLK : (k + 1) * BLK, :] = made[h, sel[k]]
@@ -166,7 +172,7 @@
                     kv_direct(h, d).start()
             kv_own(h).start()
 
-    loads[5].wait()
+    loads[6].wait()
     queries = jnp.dot(tok[...].reshape(n_rows, -1), wq[...], preferred_element_type=F32) * SCALE
     for h in range(nh):
         two = queries[:, (h // 2) * BLK : (h // 2 + 1) * BLK]
@@ -177,18 +183,22 @@
     loads[1].wait()
     make_bias(mask_v, band, nb, bias)
     tq = n_rows // 2
+    far = (z * 2) // nz
+
+    def part(i):
+        return pl.ds(pl.multiple_of(lax.rem(i + 1 + far, 2) * tq, tq), tq)
 
     def span(b):
         return pl.ds(pl.multiple_of(b * W, W), W)
 
     def score(h, b, i):
-        r = slice(i * tq, (i + 1) * tq)
+        r = part(i)
         q = jnp.concatenate([q_pad[h, r, :], bias[r, :]], axis=1)
         k = jnp.concatenate([kv[h, b], onehot[span(b), :]], axis=1)
         return lax.dot_general(q, k, NT, preferred_element_type=F32)
 
     def gather(s, h, b, i, first):
-        r = slice(i * tq, (i + 1) * tq)
+        r = part(i)
         cut = [s[:, j * BLK : (j + 1) * BLK] for j in range(KEEP)]
         m = jnp.broadcast_to(functools.reduce(jnp.maximum, cut).max(axis=1, keepdims=True), (tq, BLK))
         if not first:
@@ -203,12 +213,14 @@
             a = a + acc[h, r, :] * jnp.exp2(before - m)
         acc[h, r, :] = a
 
-    def block(h, bands, first):
+    def block(h, bands, first, done=None):
         units = [(b, i, first and n == 0) for n, b in enumerate(bands) for i in range(2)]
         s = score(h, *units[0][:2])
         for n, (b, i, start) in enumerate(units):
             after = score(h, *units[n + 1][:2]) if n + 1 < len(units) else None
             gather(s, h, b, i, start)
+            if done is not None:
+                done(i)
             s = after
 
     def local_block(h, _):
@@ -230,6 +242,19 @@
     def a_arrived(h, d):
         origin = lax.rem(z + d, nz)
         remote(att.at[h, origin], got.at[h, origin], a_send.at[h, d], a_recv.at[h, origin], {"head": origin}).wait_recv()
+
+    reach = nz // 2
+
+    def finish(h, i):
+        base = lax.rem(far + 1 + i, 2) * reach
+        order = [lax.rem(z + e, reach) + base for e in range(reach)]
+        for p in order:
+            lo = p * 2 * half
+            a0 = acc[h, pl.ds(pl.multiple_of(lo, half), half), :]
+            a1 = acc[h, pl.ds(pl.multiple_of(lo + half, half), half), :]
+            value = jnp.where(low_half, pltpu.roll(a0, HD, 1), a1)
+            mass = jnp.where(low_half, a0, pltpu.roll(a1, HD, 1))
+            att[h, p] = (value / mass).astype(BF16)
 
     def far_block(h, _):
         @pl.when(h == 1)
@@ -245,13 +270,7 @@
             kv_forward(h, d).start()
             block(h, (same,), False)
             kv_arrived(h, chip_at(d) * 2 + 1 - core)
-            block(h, (chip_at(d) * 2 + 1 - core,), False)
-        for p in range(nz):
-            a0 = acc[h, p * 2 * half : p * 2 * half + half, :]
-            a1 = acc[h, p * 2 * half + half : (p + 1) * 2 * half, :]
-            value = jnp.where(low_half, pltpu.roll(a0, HD, 1), a1)
-            mass = jnp.where(low_half, a0, pltpu.roll(a1, HD, 1))
-            att[h, p] = (value / mass).astype(BF16)
+            block(h, (chip_at(d) * 2 + 1 - core,), False, functools.partial(finish, h) if d == n_chips - 1 else None)
         for d in range(1, nz):
             a_copy(h, d).start()
         got[h, z] = att[h, z]
@@ -266,7 +285,7 @@
     for t in range(nt):
         for d in range(1, nz):
             w_arrived(d, lax.rem(tile + t, nt) * 2 + 1 - core)
-    loads[6].wait()
+    loads[7].wait()
 
     def heads(hs):
         return jnp.concatenate(
@@ -336,7 +355,7 @@
             vmem((nh, nz, out_rows // 2, 2 * HD), BF16),
             vmem((nz,) + w_out.shape, BF16),
             vmem((out_rows, w_out.shape[1]), F32),
-            dma((7,)),
+            dma((8,)),
             dma((nh, nb // 2)),
             dma((nh, nb // 2)),
             dma((nh, nb)),

time: 35.6 us -> 35 us (0.983)
  Pallas kernels: 33.8 us -> 33.2 us
    pallas_call x1, Pallas kernels: 33.8 us -> 33.2 us  [on_device(): pl.pallas_call(functools.partial(layer, nt, nb, nz), out_shape=jax.ShapeD...]
where the time goes in v3:
time: 35 us; the launch traced here: 34.8 us
  Pallas kernels  33.2 us (95%)
  local copies, waits for them, and re-layouts  1.51 us (4%)
    pallas_call x1, Pallas kernels, on_device(): pl.pallas_call(functools.partial(layer, nt, nb, nz), out_shape=jax.ShapeD...  33.2 us
    unnamed x3, local copies, waits for them, and re-layouts  1.51 us

profile of v3, /device:TPU:0, one launch (start us, length us, event | category | flops | bytes accessed | tf_op | source)
XLA Modules:
  0.0 34.8 jit_solution(2701825614103464099)
XLA Ops:
  0.0 0.0 copy-start
  0.0 0.7 %copy-done = s32[32,32]{1,0:T(8,128)S(1)} copy-done((s32[32,32]{1,0:T(8,128)S(1)}, s32[32,32]{1,0:T(8,128)}, u32[]{:S(2)}) %copy-start) | copy-done | bytes 4120
  0.7 33.2 %layer.1 = bf16[256,1024]{1,0:T(8,128)(2,1)S(1)} custom-call(s32[32,32]{1,0:T(8,128)S(1)} %copy-done, bf16[8,128,1024]{2,1,0:T(8,128)(2,1)} %bitcast.1, bf16[1024,256]{1,0:T(8,128)(2,1)} %wq_h.1, bf16[1024,256]{1,0:T(8,128)(2,1)} %wk_h.1, bf16[1024,256]{1,0:T(8,128)(2,1)} %wv_h.1, bf16[256,1024]{1,0:T(8,128)(2,1)} %wo_h.1), custom_call_target="tpu_custom_call" | custom-call | tf_op jit(solution)/shard_map/layer/pallas_call | solution.py:335
  34.0 0.8 %copy.8 = bf16[256,1024]{1,0:T(8,128)(2,1)} copy(bf16[256,1024]{1,0:T(8,128)(2,1)S(1)} %layer.1) | data formatting | bytes 1048576
Async XLA Ops:
  0.0 0.7 %copy-start = (s32[32,32]{1,0:T(8,128)S(1)}, s32[32,32]{1,0:T(8,128)}, u32[]{:S(2)}) copy-start(s32[32,32]{1,0:T(8,128)} %mask_h.1) | copy-start | bytes 12292

commit v4 on v3

--- a/solution.py
+++ b/solution.py
@@ -233,8 +233,6 @@
         block(h, (band, sibling), True)
         return 0
 
-    lax.fori_loop(0, nh, local_block, 0)
-
     def a_copy(h, d):
         to = lax.rem(z + d, nz)
         return remote(att.at[h, to], got.at[h, z], a_send.at[h, d], a_recv.at[h, z], {"head": to})
@@ -276,7 +274,18 @@
         got[h, z] = att[h, z]
         return 0
 
-    lax.fori_loop(0, nh, far_block, 0)
+    def turn(i, _):
+        @pl.when(i < nh)
+        def _():
+            local_block(i, 0)
+
+        @pl.when(i >= 2)
+        def _():
+            far_block(i - 2, 0)
+
+        return 0
+
+    lax.fori_loop(0, nh + 2, turn, 0)
 
     for t in range(1, nt):
         for d in range(1, nz):

time: 35 us -> 35 us (level)
  no operation moved by 1% of the time
where the time goes in v4:
time: 35 us; the launch traced here: 34.8 us
  Pallas kernels  33.2 us (95%)
  local copies, waits for them, and re-layouts  1.51 us (4%)
    pallas_call x1, Pallas kernels, on_device(): pl.pallas_call(functools.partial(layer, nt, nb, nz), out_shape=jax.ShapeD...  33.2 us
    unnamed x3, local copies, waits for them, and re-layouts  1.51 us

profile of v4, /device:TPU:0, one launch (start us, length us, event | category | flops | bytes accessed | tf_op | source)
XLA Modules:
  0.0 34.8 jit_solution(12858250369457059332)
XLA Ops:
  0.0 0.0 copy-start
  0.0 0.7 %copy-done = s32[32,32]{1,0:T(8,128)S(1)} copy-done((s32[32,32]{1,0:T(8,128)S(1)}, s32[32,32]{1,0:T(8,128)}, u32[]{:S(2)}) %copy-start) | copy-done | bytes 4120
  0.7 33.2 %layer.1 = bf16[256,1024]{1,0:T(8,128)(2,1)S(1)} custom-call(s32[32,32]{1,0:T(8,128)S(1)} %copy-done, bf16[8,128,1024]{2,1,0:T(8,128)(2,1)} %bitcast.1, bf16[1024,256]{1,0:T(8,128)(2,1)} %wq_h.1, bf16[1024,256]{1,0:T(8,128)(2,1)} %wk_h.1, bf16[1024,256]{1,0:T(8,128)(2,1)} %wv_h.1, bf16[256,1024]{1,0:T(8,128)(2,1)} %wo_h.1), custom_call_target="tpu_custom_call" | custom-call | tf_op jit(solution)/shard_map/layer/pallas_call | solution.py:344
  34.0 0.8 %copy.8 = bf16[256,1024]{1,0:T(8,128)(2,1)} copy(bf16[256,1024]{1,0:T(8,128)(2,1)S(1)} %layer.1) | data formatting | bytes 1048576
Async XLA Ops:
  0.0 0.7 %copy-start = (s32[32,32]{1,0:T(8,128)S(1)}, s32[32,32]{1,0:T(8,128)}, u32[]{:S(2)}) copy-start(s32[32,32]{1,0:T(8,128)} %mask_h.1) | copy-start | bytes 12292

commit v5 on v4

--- a/solution.py
+++ b/solution.py
@@ -76,9 +76,6 @@
              (tok_h.at[: nq // 2], tok.at[: nq // 2]), (tok_h.at[nq // 2 :], tok.at[nq // 2 :]),
              (wq_h, wq), (wo_h, wo.at[z]))
     loads = [pltpu.make_async_copy(a, b, load.at[i]) for i, (a, b) in enumerate(pairs)]
-    for c in loads:
-        c.start()
-
     def chip_at(step):
         return lax.rem(chip + step, n_chips)
 
@@ -89,6 +86,8 @@
     barrier = pltpu.get_barrier_semaphore()
     for p in peers:
         pl.semaphore_signal(barrier, inc=1, device_id=p, device_id_type=mesh_id)
+    for c in loads:
+        c.start()
 
     def remote(src, dst, send, recv, to):
         return pltpu.make_async_remote_copy(
@@ -136,9 +135,6 @@
         piece = w_piece(source, part)
         remote(piece, piece, w1_send.at[d], w_recv.at[source, part], {"band": sibling}).wait_recv()
 
-    slot_of = lax.broadcasted_iota(I32, (BLK, slots), 1)
-    for s in range(nb * KEEP):
-        onehot[s * BLK : (s + 1) * BLK, :] = jnp.where(slot_of == s, 1.0, 0.0).astype(BF16)
     loads[0].wait()
     sel = select_blocks(mask_s, band, nq)
     pl.semaphore_wait(barrier, len(peers))
@@ -180,6 +176,9 @@
             two = pltpu.roll(two, HD, 1)
         q_pad[h] = jnp.where(low_half, two, 0.0).astype(BF16)
 
+    slot_of = lax.broadcasted_iota(I32, (BLK, slots), 1)
+    for s in range(nb * KEEP):
+        onehot[s * BLK : (s + 1) * BLK, :] = jnp.where(slot_of == s, 1.0, 0.0).astype(BF16)
     loads[1].wait()
     make_bias(mask_v, band, nb, bias)
     tq = n_rows // 2

time: 35 us -> 35 us (level)
  no operation moved by 1% of the time
where the time goes in v5:
time: 35 us; the launch traced here: 34.8 us
  Pallas kernels  33.2 us (95%)
  local copies, waits for them, and re-layouts  1.51 us (4%)
    pallas_call x1, Pallas kernels, on_device(): pl.pallas_call(functools.partial(layer, nt, nb, nz), out_shape=jax.ShapeD...  33.2 us
    unnamed x3, local copies, waits for them, and re-layouts  1.51 us

profile of v5, /device:TPU:0, one launch (start us, length us, event | category | flops | bytes accessed | tf_op | source)
XLA Modules:
  0.0 34.8 jit_solution(14771956588527910362)
XLA Ops:
  0.0 0.0 copy-start
  0.0 0.7 %copy-done = s32[32,32]{1,0:T(8,128)S(1)} copy-done((s32[32,32]{1,0:T(8,128)S(1)}, s32[32,32]{1,0:T(8,128)}, u32[]{:S(2)}) %copy-start) | copy-done | bytes 4120
  0.7 33.2 %layer.1 = bf16[256,1024]{1,0:T(8,128)(2,1)S(1)} custom-call(s32[32,32]{1,0:T(8,128)S(1)} %copy-done, bf16[8,128,1024]{2,1,0:T(8,128)(2,1)} %bitcast.1, bf16[1024,256]{1,0:T(8,128)(2,1)} %wq_h.1, bf16[1024,256]{1,0:T(8,128)(2,1)} %wk_h.1, bf16[1024,256]{1,0:T(8,128)(2,1)} %wv_h.1, bf16[256,1024]{1,0:T(8,128)(2,1)} %wo_h.1), custom_call_target="tpu_custom_call" | custom-call | tf_op jit(solution)/shard_map/layer/pallas_call | solution.py:343
  34.0 0.8 %copy.8 = bf16[256,1024]{1,0:T(8,128)(2,1)} copy(bf16[256,1024]{1,0:T(8,128)(2,1)S(1)} %layer.1) | data formatting | bytes 1048576
Async XLA Ops:
  0.0 0.7 %copy-start = (s32[32,32]{1,0:T(8,128)S(1)}, s32[32,32]{1,0:T(8,128)}, u32[]{:S(2)}) copy-start(s32[32,32]{1,0:T(8,128)} %mask_h.1) | copy-start | bytes 12292
